TPU v7x, 32 devices: a whole 2x2x4 slice. The times are simulated.
32 devices in a mesh: grp: 2 (over x), blk: 16 (over z, y, core).
Axes of the slice: x: 2, y: 2, z: 4, core: 2. Of those that a mesh axis runs over, the one named last changes fastest.
Arguments:
- query_sketch: bfloat16 [16384, 4096], P(('grp', 'blk')), parts along dimension 0, may hold values from -6 to 6
- train_sketch: bfloat16 [4096, 4096], P(('grp', 'blk')), parts along dimension 0, may hold values from -6 to 6
- train_ids: int32 [4096], P(('grp', 'blk')), parts along dimension 0, may hold values from 0 to 2047, each once
- basis_in: bfloat16 [64, 64], P('blk'), may hold values from -0.75 to 0.75
- basis_out: bfloat16 [64, 64], P('blk'), may hold values from -0.75 to 0.75
- eig_in: float32 [64], replicated, may hold values from 0.3 to 3
- eig_out: float32 [64], replicated, may hold values from 0.3 to 3
Outputs:
- scores: float32 [16384, 2048], P(('grp', 'blk')), parts along dimension 0
- totals: float32 [4096], P(('grp', 'blk')), parts along dimension 0
There are 2 independent parts, one for each index of `grp`. A program takes and returns all parts, laid end to end along the dimension named above; an argument that names none is the same for every part. Nothing has to cross between parts.
Inputs may be any that keep to these rules, and one draw needn't show every extreme that they name: `train_ids`: each id appears once in a group.
All inputs are finite; a program needn't handle non-finite values.
Results may differ from a plain program's by a relative error of at most 0.0042.
Values may be sent and summed in bfloat16 or wider, within the bound.
A program may use at most 192 MiB of HBM per device.

v0:
```python
import jax
import jax.numpy as jnp
from jax import lax
from jax.sharding import PartitionSpec as P

FOUT = 64
FIN = 64


def rotate(sketch, factor_in, factor_out):
    rows = sketch.shape[0]
    grid = sketch.reshape(rows, FOUT, FIN)
    half = jnp.einsum("rof,fi->roi", grid, factor_in, preferred_element_type=jnp.float32).astype(
        jnp.bfloat16
    )
    turned = jnp.einsum("op,roi->rpi", factor_out, half, preferred_element_type=jnp.float32)
    return turned.reshape(rows, FOUT * FIN)


def against(query_rot, block_rot):
    return lax.dot_general(
        query_rot, block_rot, (((1,), (1,)), ((), ())), preferred_element_type=jnp.float32
    )


def per_device(query_sketch, train_sketch, train_ids, basis_in, basis_out, eig_in, eig_out):
    factor_in, factor_out = (
        lax.all_gather(basis_in, "blk", axis=0, tiled=True),
        lax.all_gather(basis_out, "blk", axis=0, tiled=True),
    )
    all_ids = lax.all_gather(train_ids, "blk", axis=0, tiled=True)
    width = FOUT * FIN
    eigen_grid = (eig_out[:, None] * eig_in[None, :] + 0.01).reshape(width)
    query_rot = (
        rotate(query_sketch, factor_in, factor_out) / eigen_grid / jnp.sqrt(jnp.float32(width))
    ).astype(jnp.bfloat16)
    scores = against(
        query_rot,
        rotate(
            lax.all_gather(train_sketch, "blk", axis=0, tiled=True), factor_in, factor_out
        ).astype(jnp.bfloat16),
    )
    devices = lax.axis_size("blk")
    queries_all = query_sketch.shape[0] * devices
    column_sums = jnp.sum(scores, axis=0) / jnp.sqrt(jnp.float32(queries_all))
    by_id = jnp.zeros(column_sums.shape, jnp.float32).at[all_ids].set(column_sums)
    totals = lax.psum_scatter(by_id, "blk", scatter_dimension=0, tiled=True)
    return (scores, totals)


def solution(mesh):
    placed = (
        P(("grp", "blk"), None),
        P(("grp", "blk"), None),
        P(("grp", "blk")),
        P("blk", None),
        P("blk", None),
        P(),
        P(),
    )
    return jax.shard_map(
        per_device,
        mesh=mesh,
        in_specs=placed,
        out_specs=(P(("grp", "blk"), None), P(("grp", "blk"))),
        check_vma=False,
    )
```

profile of v0, /device:TPU:0, one launch (start us, length us, event | category | flops | bytes accessed | tf_op | source)
XLA Modules:
  0.0 235.0 jit_solution(612312419529073752)
XLA Ops:
  7.2 0.0 copy-start.5
  7.2 0.0 copy-start
  7.2 0.0 copy-start.1
  7.2 0.0 copy-start.4
  7.2 0.0 copy-start.2
  7.2 0.0 copy-start.3
  7.2 0.0 all-gather.5.cloned.1.call-start
  7.3 2.3 copy.23
  9.5 0.0 all-gather.5.cloned.1.call-update
  9.6 6.4 %copy.19 = bf16[512,4096]{0,1:T(8,128)(2,1)} copy(bf16[512,4096]{1,0:T(8,128)(2,1)} %param.7) | data formatting | bytes 8388608 | tf_op args[0]
  16.0 0.0 copy-done.5
  16.0 0.6 dynamic-slice
  17.2 0.0 copy-done
  17.2 23.3 %all-gather.1 = bf16[16,4,64]{2,1,0:T(4,128)(2,1)S(1)} all-gather(bf16[1,4,64]{2,1,0:T(4,128)(2,1)S(1)} %bitcast.48), channel_id=1, replica_groups=mesh['grp'=2,'blk'=16] {'blk'}, dimensions={0}, use_global_device_ids=true | all-gather | bytes 8704 | tf_op jit(solution)/shard_map/all_gather | solution.py:29
  40.5 0.0 copy-done.1
  40.5 17.5 %all-gather = bf16[16,4,64]{2,1,0:T(4,128)(2,1)S(1)} all-gather(bf16[1,4,64]{2,1,0:T(4,128)(2,1)S(1)} %bitcast.49), channel_id=1, replica_groups=mesh['grp'=2,'blk'=16] {'blk'}, dimensions={0}, use_global_device_ids=true | all-gather | bytes 8704 | tf_op jit(solution)/shard_map/all_gather | solution.py:28
  58.1 0.0 copy-done.4
  58.1 18.9 %all-gather.2 = s32[16,1,128]{2,1,0:T(1,128)S(1)} all-gather(s32[1,1,128]{2,1,0:T(1,128)S(1)} %bitcast.50), channel_id=1, replica_groups=mesh['grp'=2,'blk'=16] {'blk'}, dimensions={0}, use_global_device_ids=true | all-gather | bytes 8704 | tf_op jit(solution)/shard_map/all_gather | solution.py:31
  76.9 0.0 copy-done.2
  77.0 0.0 copy-done.3
  77.0 0.1 multiply_add_fusion
  77.0 3.5 %convolution_convert_fusion.1 = bf16[512,64,64]{0,2,1:T(8,128)(2,1)S(1)} fusion(bf16[512,64,64]{0,2,1:T(8,128)(2,1)} %bitcast.42, bf16[64,64,1]{1,0,2:T(8,128)(2,1)S(1)} %bitcast.43), kind=kOutput, calls=%fused_computation.15 | convolution fusion | flops 270532608 | bytes 8396800 | tf_op jit(solution)/shard_map/rof,fi->roi/dot_general | solution.py:13
  80.5 6.6 %fusion.12 = f32[512,64,64]{0,2,1:T(8,128)} fusion(bf16[64,64,1]{1,0,2:T(8,128)(2,1)S(1)} %bitcast.45, bf16[512,64,64]{0,2,1:T(8,128)(2,1)S(1)} %convolution_convert_fusion.1), kind=kOutput, calls=%fused_computation.10 | convolution fusion | flops 268435456 | bytes 12591104 | tf_op jit(solution)/shard_map/op,roi->rpi/dot_general | solution.py:16
  87.1 56.5 %all-gather.5.cloned.1.call-done = bf16[2048,4096]{0,1:T(8,128)(2,1)} async-done(((bf16[128,4096]{0,1:T(8,128)(2,1)}), bf16[2048,4096]{0,1:T(8,128)(2,1)}) %all-gather.5.cloned.1.call-update) | async-done | bytes 16777232 | tf_op jit(solution)/shard_map/all_gather | solution.py:40
  143.6 12.5 %convolution_convert_fusion = bf16[2048,64,64]{0,2,1:T(8,128)(2,1)} fusion(bf16[2048,64,64]{0,2,1:T(8,128)(2,1)} %bitcast.41, bf16[64,64,1]{1,0,2:T(8,128)(2,1)S(1)} %bitcast.44), kind=kOutput, calls=%fused_computation.6 | convolution fusion | flops 1082130432 | bytes 33562624 | tf_op jit(solution)/shard_map/rof,fi->roi/dot_general | solution.py:13
  156.1 31.4 %fusion.26 = (f32[2048]{0:T(1024)S(1)}, f32[512,2048]{1,0:T(8,128)}) fusion(bf16[64,64,1]{1,0,2:T(8,128)(2,1)S(1)} %bitcast.46, bf16[2048,64,64]{0,2,1:T(8,128)(2,1)} %convolution_convert_fusion, f32[512,64,64]{0,2,1:T(8,128)} %fusion.12, f32[64,64]{0,1:T(8,128)S(1)} %multiply_add_fusion), kind=kOutput, calls=%fused_computation.22 | convolution fusion | flops 9679403008 | bytes 29392896 | tf_op jit(solution)/shard_map/dot_general | solution.py:21
  187.5 8.0 %scatter_custom_fusion = f32[2048]{0:T(1024)S(1)} fusion(s32[2048]{0:T(1024)S(1)} %compare_select_fusion, f32[2048]{0:T(1024)S(1)} %broadcast_multiply_fusion, f32[]{:T(128)} %constant.3.clone.1), kind=kCustom, calls=%fused_computation.19 | custom fusion | bytes 8196 | tf_op jit(solution)/shard_map/scatter | solution.py:46
  195.6 32.0 %all-reduce = f32[2048]{0:T(1024)S(1)} all-reduce(f32[2048]{0:T(1024)S(1)} %scatter_custom_fusion), channel_id=2, replica_groups=mesh['grp'=2,'blk'=16] {'blk'}, use_global_device_ids=true, to_apply=%region_2.0.clone | all-reduce | flops 2048 | bytes 16384
  227.6 0.6 dynamic-slice.1
  (2 shorter events, 0.0 us)
Async XLA Ops:
  7.2 8.8 %copy-start.5 = (u32[32]{0:T(128)S(1)}, u32[32]{0:T(128)}, u32[]{:S(2)}) copy-start(u32[32]{0:T(128)} %constant.19) | copy-start | bytes 388
  7.2 10.1 %copy-start = (bf16[4,64]{1,0:T(4,128)(2,1)S(1)}, bf16[4,64]{1,0:T(4,128)(2,1)}, u32[]{:S(2)}) copy-start(bf16[4,64]{1,0:T(4,128)(2,1)} %param.11) | copy-start | bytes 1540
  7.2 33.4 %copy-start.1 = (bf16[4,64]{1,0:T(4,128)(2,1)S(1)}, bf16[4,64]{1,0:T(4,128)(2,1)}, u32[]{:S(2)}) copy-start(bf16[4,64]{1,0:T(4,128)(2,1)} %param.10) | copy-start | bytes 1540
  7.2 50.9 %copy-start.4 = (s32[128]{0:T(128)S(1)}, s32[128]{0:T(128)}, u32[]{:S(2)}) copy-start(s32[128]{0:T(128)} %param.9) | copy-start | bytes 1540
  7.2 69.7 %copy-start.2 = (f32[64]{0:T(128)S(1)}, f32[64]{0:T(128)}, u32[]{:S(2)}) copy-start(f32[64]{0:T(128)} %param.12) | copy-start | bytes 772
  7.2 69.7 %copy-start.3 = (f32[64]{0:T(128)S(1)}, f32[64]{0:T(128)}, u32[]{:S(2)}) copy-start(f32[64]{0:T(128)} %param.13) | copy-start | bytes 772
  7.2 136.3 %all-gather.5.cloned.1.call-start = ((), (), s32[]{:S(2)}) async-start(), calls=%async_computation | async-start | bytes 17825792 | tf_op jit(solution)/shard_map/all_gather | solution.py:40
Sparse Core Ops, SparseCore 0:
  10.2 133.2 all-gather.4
where the time goes:
time: 235 us
  blocking collectives  91.7 us (39%)
  waiting for transfers between devices  56.5 us (24%)
  matrix products  54 us (23%)
  local copies, waits for them, and re-layouts  17.9 us (8%)
  between operations  14.8 us (6%)
    all_gather x1, waiting for transfers between devices, per_device(): lax.all_gather(train_sketch, 'blk', axis=0, tiled=True)  56.5 us
    unnamed x1, blocking collectives  32 us
    dot_general x1, matrix products, against(): lax.dot_general(query_rot, block_rot, (((1,), (1,)), ((), ())), preferred...  31.4 us
    all_gather x1, blocking collectives, per_device(): lax.all_gather(basis_out, 'blk', axis=0, tiled=True)  23.3 us
    all_gather x1, blocking collectives, per_device(): all_ids = lax.all_gather(train_ids, 'blk', axis=0, tiled=True)  18.9 us
    all_gather x1, blocking collectives, per_device(): lax.all_gather(basis_in, 'blk', axis=0, tiled=True)  17.5 us
    dot_general x2, matrix products, rotate(): jnp.einsum('rof,fi->roi', grid, factor_in, preferred_element_type=jnp.flo...  16 us
    unnamed x16, local copies, waits for them, and re-layouts  9.88 us
  transfers between devices with their start and end apart: 1, of which 1 were waited for; matrix products, arithmetic and copies ran while one was open for 7% of the time, Pallas kernels for 0%

commit v1 on v0

v1 whole, which is shorter than its diff:
```python
import functools

import jax
import jax.numpy as jnp
from jax import lax
from jax.experimental import pallas as pl
from jax.experimental.pallas import tpu as pltpu
from jax.sharding import PartitionSpec as P

FOUT = 64
FIN = 64
LANES = 256
CHUNKS = 4
ITEMS = 4

MESH = pl.DeviceIdType.MESH
BF16 = jnp.bfloat16
F32 = jnp.float32


def dot(a, b, dims=((1,), (0,))):
    return lax.dot_general(a, b, (dims, ((), ())), preferred_element_type=F32)


NT = ((1,), (1,))


def kernel(
    n, lines, q_ref, t_ref, small_ref, scale_ref, scores_ref, totals_ref,
    held, qa, qb, wcol, spread, block_in, stage, factors, smalls, qsum, csum,
    recv, sends, small_recv, small_send, qsum_recv, qsum_send, csum_recv, csum_send,
    local_sem, out_sem,
):
    depth = n // (2 * lines)
    rows = t_ref.shape[0]
    width = t_ref.shape[1]
    piece = rows // CHUNKS
    crossed = CHUNKS // 2 if lines == 2 else 0
    groups = width // LANES
    per = small_ref.shape[0]
    basis_rows = FIN // n
    queries = q_ref.shape[0] * n
    slots = depth * CHUNKS
    spin = 2 * groups // ITEMS

    me = lax.axis_index("blk")
    c = lax.rem(me, 2)
    y = lax.rem(lax.div(me, 2), lines)
    z = lax.div(me, 2 * lines)

    def index(z0, y0, c0):
        return (z0 * lines + y0) * 2 + c0

    q_copy = pltpu.make_async_copy(q_ref, qa, local_sem.at[0])
    q_copy.start()
    own_copy = pltpu.make_async_copy(
        t_ref, held.at[pl.ds(pl.multiple_of(me * rows, rows), rows), :], local_sem.at[1]
    )
    own_copy.start()

    barrier = pltpu.get_barrier_semaphore()

    @pl.loop(1, n)
    def _(j):
        pl.semaphore_signal(
            barrier, inc=1, device_id={"blk": lax.rem(me + j, n)}, device_id_type=MESH
        )

    pl.semaphore_wait(barrier, n - 1)

    def place(s, h):
        return held.at[pl.ds(pl.multiple_of(s * rows + h * piece, piece), piece), :]

    def moved(way, z0, y0, c0, h, target, own=False):
        spot = place(index(z0, y0, c0), h)
        src = t_ref.at[pl.ds(pl.multiple_of(h * piece, piece), piece), :] if own else spot
        return pltpu.make_async_remote_copy(
            src_ref=src,
            dst_ref=spot,
            send_sem=sends.at[way, (z0 * lines + y0) * CHUNKS + h],
            recv_sem=recv.at[index(z0, y0, c0) * CHUNKS + h],
            device_id={"blk": target},
            device_id_type=MESH,
        )

    def ways(z0, y0, h):
        same = y0 == y
        here = jnp.logical_and(y0 != y, jnp.logical_and(z0 == z, h < crossed))
        up = jnp.logical_and(z + 1 < depth, jnp.logical_or(jnp.logical_and(same, z0 <= z), here))
        down = jnp.logical_and(z > 0, jnp.logical_or(jnp.logical_and(same, z0 >= z), here))
        near = jnp.logical_or(z0 == z + 1, z0 == z - 1)
        over = jnp.logical_and(same, jnp.logical_not(jnp.logical_and(near, h < crossed)))
        return up, down, over

    up_target = index(jnp.minimum(z + 1, depth - 1), y, c)
    down_target = index(jnp.maximum(z - 1, 0), y, c)
    over_target = index(z, lines - 1 - y, c)
    twin = index(z, y, 1 - c)

    def send_z(z0, y0, h, own=False):
        up, down, _ = ways(z0, y0, h)

        @pl.when(up)
        def _():
            moved(0, z0, y0, c, h, up_target, own).start()

        @pl.when(down)
        def _():
            moved(1, z0, y0, c, h, down_target, own).start()

    def send_y(z0, y0, h, own=False):
        if lines == 2:

            @pl.when(ways(z0, y0, h)[2])
            def _():
                moved(2, z0, y0, c, h, over_target, own).start()

    def send_twin(z0, y0, h, own=False):
        moved(3, z0, y0, c, h, twin, own).start()

    def arrived(z0, y0, c0, h):
        moved(3, z0, y0, c0, h, twin).wait_recv()

    def order(step):
        both = jnp.minimum(z, depth - 1 - z)
        near = z + (1 - 2 * lax.rem(step, 2)) * (lax.div(step, 2) + 1)
        toward = jnp.where(z < depth - 1 - z, 1, -1)
        return jnp.where(step < 2 * both, near, z + toward * (step - both + 1))

    def to_all(buffer, send_sem, recv_sem, j):
        return pltpu.make_async_remote_copy(
            src_ref=buffer.at[me],
            dst_ref=buffer.at[me],
            send_sem=send_sem.at[j],
            recv_sem=recv_sem.at[me],
            device_id={"blk": lax.rem(me + j, n)},
            device_id_type=MESH,
        )

    def from_one(buffer, send_sem, recv_sem, j):
        s = lax.rem(me + j, n)
        return pltpu.make_async_remote_copy(
            src_ref=buffer.at[s],
            dst_ref=buffer.at[s],
            send_sem=send_sem.at[j],
            recv_sem=recv_sem.at[s],
            device_id={"blk": s},
            device_id_type=MESH,
        )

    def share(buffer, send_sem, recv_sem):
        @pl.loop(1, n)
        def _(j):
            to_all(buffer, send_sem, recv_sem, j).start()

    def collect(buffer, send_sem, recv_sem):
        @pl.loop(1, n)
        def _(j):
            from_one(buffer, send_sem, recv_sem, j).wait_recv()
            to_all(buffer, send_sem, recv_sem, j).wait_send()

    smalls[me] = small_ref[...]
    share(smalls, small_send, small_recv)

    @pl.loop(0, CHUNKS)
    def _(h):
        send_z(z, y, h, own=True)
        send_y(z, y, h, own=True)
        send_twin(z, y, h, own=True)

    collect(smalls, small_send, small_recv)
    for s in range(n):
        factors[s * basis_rows : (s + 1) * basis_rows, :] = smalls[s, 0:basis_rows, :]
    basis_in = factors[:, 0:FIN].astype(BF16)
    basis_out = factors[:, FIN : FIN + FOUT].astype(BF16)

    def hot(test, dims):
        a = lax.broadcasted_iota(jnp.int32, dims, 0)
        b = lax.broadcasted_iota(jnp.int32, dims, 1)
        return test(a, b).astype(F32).astype(BF16)

    repeat = hot(lambda a, b: a % FIN == b, (LANES, FIN))
    alike = hot(lambda a, b: a // FIN == b // FIN, (LANES, LANES)).astype(F32)
    tall = dot(repeat, basis_in).astype(BF16)
    block_in[0] = (dot(tall, repeat, NT) * alike).astype(BF16)
    block_in[1] = (dot(repeat, tall, NT) * alike).astype(BF16)
    unit = hot(lambda a, b: a == b, (FOUT, FOUT))
    turned_out = dot(unit, basis_out, NT).astype(BF16)
    for g in range(groups):
        lanes = slice(g * LANES, (g + 1) * LANES)
        wide = hot(lambda a, b: a == (b + g * LANES) // FIN, (FOUT, LANES))
        spread[0, :, lanes] = dot(basis_out, wide)
        spread[1, :, lanes] = dot(turned_out, wide)

    q_copy.wait()

    def cols(g):
        return pl.ds(pl.multiple_of(g * LANES, LANES), LANES)

    @pl.loop(0, groups)
    def _(g):
        qb[:, cols(g)] = dot(qa[:, cols(g)], block_in[0]).astype(BF16)

    diagonal = (
        lax.broadcasted_iota(jnp.int32, (FIN, LANES), 0)
        == lax.broadcasted_iota(jnp.int32, (FIN, LANES), 1) % FIN
    )

    def fill(which, g):
        for o in range(FOUT):
            row = spread[which, o : o + 1, cols(g)]
            wcol[o * FIN : (o + 1) * FIN, :] = jnp.where(diagonal, row, 0.0).astype(BF16)

    def forward(g):
        fill(0, g)
        qa[:, cols(g)] = (dot(qb[...], wcol[...]) * scale_ref[:, cols(g)]).astype(BF16)

    def back(g):
        fill(1, g)
        middle = dot(qa[...], wcol[...]).astype(BF16)
        final = dot(middle, block_in[1]).astype(BF16)
        qb[:, cols(g)] = final
        qsum[me, :, cols(g)] = jnp.sum(final.astype(F32), axis=0, keepdims=True)

    def out_copy(gi, z0, y0):
        first = pl.multiple_of(index(z0, y0, 0) * rows, 2 * rows)
        slot = lax.rem(gi, 2)
        return pltpu.make_async_copy(
            stage.at[slot], scores_ref.at[:, pl.ds(first, 2 * rows)], out_sem.at[slot]
        )

    def score(gi, z0, y0):
        @pl.loop(0, CHUNKS)
        def _(h):
            arrived(z0, y0, 1 - c, h)

        @pl.when(gi >= 2)
        def _():
            out_copy(gi, z0, y0).wait()

        first = pl.multiple_of(index(z0, y0, 0) * rows, 2 * rows)
        stage[lax.rem(gi, 2)] = dot(qb[...], held[pl.ds(first, 2 * rows), :], NT)
        out_copy(gi, z0, y0).start()

    own_copy.wait()

    @pl.loop(0, slots)
    def _(k):
        step = lax.div(k, CHUNKS)
        h = lax.rem(k, CHUNKS)
        z_line = order(step)

        @pl.when(step < depth - 1)
        def _():
            arrived(z_line, y, c, h)
            send_z(z_line, y, h)
            send_y(z_line, y, h)
            send_twin(z_line, y, h)

        if lines == 2:
            z_cross = jnp.where(step == 0, z, order(step - 1))
            by_z = jnp.logical_and(
                jnp.logical_or(z_cross == z + 1, z_cross == z - 1), h < crossed
            )

            @pl.when(jnp.logical_not(by_z))
            def _():
                arrived(z_cross, 1 - y, c, h)
                send_twin(z_cross, 1 - y, h)

            @pl.when(k == slots - CHUNKS)
            def _():
                @pl.loop(0, crossed)
                def _(i):
                    send_z(z, 1 - y, i)

        @pl.when(k < spin // 2)
        def _():
            @pl.loop(0, ITEMS)
            def _(i):
                forward(k * ITEMS + i)

        @pl.when(jnp.logical_and(k >= spin // 2, k < spin))
        def _():
            @pl.loop(0, ITEMS)
            def _(i):
                back((k - spin // 2) * ITEMS + i)

        @pl.when(k == spin)
        def _():
            share(qsum, qsum_send, qsum_recv)

        @pl.when(k == spin + 2)
        def _():
            collect(qsum, qsum_send, qsum_recv)
            total = qsum[0]
            for s in range(1, n):
                total = total + qsum[s]
            high = total.astype(BF16)
            rest = total - high.astype(F32)
            middle = rest.astype(BF16)
            low = (rest - middle.astype(F32)).astype(BF16)
            mine = held[pl.ds(pl.multiple_of(me * rows, rows), rows), :]
            count = 16
            sums = jnp.zeros((1, rows), F32)
            for part in (low, middle, high):
                full = jnp.broadcast_to(part.astype(F32), (count, width)).astype(BF16)
                sums = sums + dot(full, mine, NT)[0:1, :]
            csum[me] = sums * (1.0 / float(queries) ** 0.5)
            share(csum, csum_send, csum_recv)

        early = k - spin
        use_own = early == 0
        use_first = jnp.logical_and(early >= 1, early <= 2)
        use_line = jnp.logical_and(
            early >= 3, jnp.logical_and(h == CHUNKS - 1, step < depth - 1)
        )
        chosen = jnp.where(use_first, early - 1, step)
        z_score = jnp.where(use_own, z, order(chosen))
        gi = jnp.where(use_own, 0, chosen + 1)
        use = jnp.logical_or(use_own, jnp.logical_or(use_first, use_line))
        y_score = y
        if lines == 2:
            use_cross = k == slots - CHUNKS
            z_score = jnp.where(use_cross, z, z_score)
            y_score = jnp.where(use_cross, 1 - y, y)
            gi = jnp.where(use_cross, depth, gi)
            use = jnp.logical_or(use, use_cross)

        @pl.when(use)
        def _():
            score(gi, z_score, y_score)

    if lines == 2:
        for side in (1, -1):

            @pl.when(jnp.logical_and(z + side >= 0, z + side < depth))
            def _():
                @pl.loop(0, crossed)
                def _(h):
                    arrived(z + side, 1 - y, c, h)
                    send_twin(z + side, 1 - y, h)

        @pl.loop(0, depth - 1)
        def _(j):
            score(depth + 1 + j, order(depth - 2 - j), 1 - y)

    collect(csum, csum_send, csum_recv)
    ids = (
        lax.broadcasted_iota(jnp.int32, (rows, rows), 0) + me * rows
    ).astype(F32)
    picked = jnp.zeros((rows, rows), F32)
    for s in range(n):
        picked = picked + jnp.where(smalls[s, per - 1 : per, :] == ids, csum[s], 0.0)
    totals_ref[...] = jnp.sum(picked.T, axis=0, keepdims=True)

    done = depth * lines
    out_copy(done, z, y).wait()
    out_copy(done + 1, z, y).wait()

    @pl.loop(0, depth * lines)
    def _(s):
        z0 = lax.div(s, lines)
        y0 = lax.rem(s, lines)

        @pl.loop(0, CHUNKS)
        def _(h):
            up, down, over = ways(z0, y0, h)

            @pl.when(up)
            def _():
                moved(0, z0, y0, c, h, up_target).wait_send()

            @pl.when(down)
            def _():
                moved(1, z0, y0, c, h, down_target).wait_send()

            if lines == 2:

                @pl.when(over)
                def _():
                    moved(2, z0, y0, c, h, over_target).wait_send()

            moved(3, z0, y0, c, h, twin).wait_send()


def per_device(n, lines, query_sketch, train_sketch, train_ids, basis_in, basis_out, eig_in, eig_out):
    width = FOUT * FIN
    queries, rows = query_sketch.shape[0], train_sketch.shape[0]
    scale = (
        1.0 / (eig_out[:, None] * eig_in[None, :] + 0.01) / jnp.sqrt(jnp.float32(width))
    ).reshape(1, width)
    both = jnp.concatenate([basis_in, basis_out], axis=1).astype(F32)
    small = jnp.concatenate(
        [both, jnp.zeros((7 - both.shape[0], 128), F32), train_ids.astype(F32)[None, :]], axis=0
    )
    sources = n // 2
    dma = pltpu.SemaphoreType.DMA
    vmem = pl.BlockSpec(memory_space=pltpu.VMEM)
    hbm = pl.BlockSpec(memory_space=pl.ANY)
    scores, totals = pl.pallas_call(
        functools.partial(kernel, n, lines),
        out_shape=(
            jax.ShapeDtypeStruct((queries, rows * n), F32),
            jax.ShapeDtypeStruct((1, rows), F32),
        ),
        in_specs=[hbm, hbm, vmem, vmem],
        out_specs=(hbm, vmem),
        scratch_shapes=[
            pltpu.VMEM((n * rows, width), BF16),
            pltpu.VMEM((queries, width), BF16),
            pltpu.VMEM((queries, width), BF16),
            pltpu.VMEM((width, LANES), BF16),
            pltpu.VMEM((2, FOUT, width), F32),
            pltpu.VMEM((2, LANES, LANES), BF16),
            pltpu.VMEM((2, queries, 2 * rows), F32),
            pltpu.VMEM((FIN, 128), F32),
            pltpu.VMEM((n, 8, 128), F32),
            pltpu.VMEM((n, 1, width), F32),
            pltpu.VMEM((n, 1, rows), F32),
            dma((n * CHUNKS,)),
            dma((4, sources * CHUNKS)),
            dma((n,)),
            dma((n,)),
            dma((n,)),
            dma((n,)),
            dma((n,)),
            dma((n,)),
            dma((2,)),
            dma((2,)),
        ],
        compiler_params=pltpu.CompilerParams(
            collective_id=0, has_side_effects=True, vmem_limit_bytes=58 * 1024 * 1024
        ),
        cost_estimate=pl.CostEstimate(
            flops=2 * queries * width * (rows * n + 2 * width),
            bytes_accessed=2 * queries * width + 4 * queries * rows * n,
            transcendentals=0,
        ),
    )(query_sketch, train_sketch, small, scale)
    return scores, totals.reshape(rows)


def solution(mesh):
    placed = (
        P(("grp", "blk"), None),
        P(("grp", "blk"), None),
        P(("grp", "blk")),
        P("blk", None),
        P("blk", None),
        P(),
        P(),
    )
    lines = 2 if mesh.shape["grp"] == 2 else 1
    return jax.shard_map(
        functools.partial(per_device, mesh.shape["blk"], lines),
        mesh=mesh,
        in_specs=placed,
        out_specs=(P(("grp", "blk"), None), P(("grp", "blk"))),
        check_vma=False,
    )
```

time: 235 us -> 121 us (0.51)
  the two profiles are of different devices: /device:TPU:0 before, /device:TPU:9 now
where the time goes in v1:
time: 121 us
  Pallas kernels  111 us (92%)
  local copies, waits for them, and re-layouts  5.98 us (5%)
  other arithmetic  2.84 us (2%)
    pallas_call x1, Pallas kernels, per_device(): pl.pallas_call(functools.partial(kernel, n, lines), out_shape=(jax.ShapeD...  111 us
    unnamed x4, local copies, waits for them, and re-layouts  5.21 us

profile of v1, /device:TPU:9, one launch (start us, length us, event | category | flops | bytes accessed | tf_op | source)
XLA Modules:
  0.0 120.7 jit_solution(8993730372869861996)
XLA Ops:
  0.6 0.7 convert_bitcast_fusion
  1.3 0.1 pad.1.clone
  1.4 0.8 maximum_convert_fusion
  2.1 0.7 pad_maximum_fusion.small_ref
  2.8 0.8 divide_multiply_fusion
  3.6 0.7 div.26.scale_ref
  4.2 111.2 %shard_map.86 = (f32[512,2048]{1,0:T(8,128)}, f32[1,128]{1,0:T(1,128)}) custom-call(bf16[512,4096]{1,0:T(8,128)(2,1)} %q_ref.1, bf16[128,4096]{1,0:T(8,128)(2,1)} %t_ref.1, f32[8,128]{1,0:T(8,128)} %pad_maximum_fusion.small_ref, f32[1,4096]{1,0:T(1,128)} %div.26.scale_ref), custom_call_target="tpu_custom_call" | custom-call | flops 42949672960 | bytes 8388608 | tf_op jit(solution)/shard_map/pallas_call | solution.py:401
  115.5 0.0 copy-start
  115.5 4.7 %copy.11 = f32[512,2048]{1,0:T(8,128)} copy(f32[512,2048]{1,0:T(8,128)} %get-tuple-element.8) | data formatting | bytes 8388608
  120.2 0.0 copy-done
  120.2 0.5 copy.12
  (1 shorter events, 0.0 us)
Async XLA Ops:
  115.5 4.7 %copy-start = (f32[1,128]{1,0:T(1,128)S(1)}, f32[1,128]{1,0:T(1,128)}, u32[]{:S(2)}) copy-start(f32[1,128]{1,0:T(1,128)} %get-tuple-element.5) | copy-start | bytes 1540

commit v2 on v1

--- a/solution.py
+++ b/solution.py
@@ -26,9 +26,10 @@
 
 
 def kernel(
-    n, lines, q_ref, t_ref, small_ref, scale_ref, scores_ref, totals_ref,
-    held, qa, qb, wcol, spread, block_in, stage, factors, smalls, qsum, csum,
-    recv, sends, small_recv, small_send, qsum_recv, qsum_send, csum_recv, csum_send,
+    n, lines, q_ref, t_ref, in_ref, out_ref, ids_ref, eig_in_ref, eig_out_ref, scores_ref, totals_ref,
+    held, qa, qb, wcol, spread, scale, block_in, stage, factors, smalls, qsum, qpart, qtotal, csum,
+    recv, sends, small_recv, small_send, qpart_recv, qpart_send, qsum_recv, qsum_send, csum_recv,
+    csum_send,
     local_sem, out_sem,
 ):
     depth = n // (2 * lines)
@@ -37,7 +38,8 @@
     piece = rows // CHUNKS
     crossed = CHUNKS // 2 if lines == 2 else 0
     groups = width // LANES
-    per = small_ref.shape[0]
+    per = smalls.shape[1]
+    slab = width // n
     basis_rows = FIN // n
     queries = q_ref.shape[0] * n
     slots = depth * CHUNKS
@@ -121,11 +123,8 @@
     def arrived(z0, y0, c0, h):
         moved(3, z0, y0, c0, h, twin).wait_recv()
 
-    def order(step):
-        both = jnp.minimum(z, depth - 1 - z)
-        near = z + (1 - 2 * lax.rem(step, 2)) * (lax.div(step, 2) + 1)
-        toward = jnp.where(z < depth - 1 - z, 1, -1)
-        return jnp.where(step < 2 * both, near, z + toward * (step - both + 1))
+    def inside(z0):
+        return jnp.logical_and(z0 >= 0, z0 < depth)
 
     def to_all(buffer, send_sem, recv_sem, j):
         return pltpu.make_async_remote_copy(
@@ -159,7 +158,10 @@
             from_one(buffer, send_sem, recv_sem, j).wait_recv()
             to_all(buffer, send_sem, recv_sem, j).wait_send()
 
-    smalls[me] = small_ref[...]
+    smalls[me] = jnp.zeros(smalls.shape[1:], F32)
+    smalls[me, 0:basis_rows, 0:FIN] = in_ref[...].astype(F32)
+    smalls[me, 0:basis_rows, FIN : FIN + FOUT] = out_ref[...].astype(F32)
+    smalls[me, per - 1 : per, :] = ids_ref[...].astype(F32)
     share(smalls, small_send, small_recv)
 
     @pl.loop(0, CHUNKS)
@@ -168,6 +170,9 @@
         send_y(z, y, h, own=True)
         send_twin(z, y, h, own=True)
 
+    for o in range(FOUT):
+        grid = eig_out_ref[0, o] * eig_in_ref[...] + 0.01
+        scale[:, o * FIN : (o + 1) * FIN] = 1.0 / grid / (float(width) ** 0.5)
     collect(smalls, small_send, small_recv)
     for s in range(n):
         factors[s * basis_rows : (s + 1) * basis_rows, :] = smalls[s, 0:basis_rows, :]
@@ -213,34 +218,49 @@
 
     def forward(g):
         fill(0, g)
-        qa[:, cols(g)] = (dot(qb[...], wcol[...]) * scale_ref[:, cols(g)]).astype(BF16)
+        qa[:, cols(g)] = (dot(qb[...], wcol[...]) * scale[:, cols(g)]).astype(BF16)
 
     def back(g):
         fill(1, g)
         middle = dot(qa[...], wcol[...]).astype(BF16)
         final = dot(middle, block_in[1]).astype(BF16)
         qb[:, cols(g)] = final
-        qsum[me, :, cols(g)] = jnp.sum(final.astype(F32), axis=0, keepdims=True)
-
-    def out_copy(gi, z0, y0):
+        column = jnp.sum(final.astype(F32), axis=0, keepdims=True)
+        for i in range(LANES // slab):
+            qsum[g * (LANES // slab) + i] = column[:, i * slab : (i + 1) * slab]
+
+    def part_to(j):
+        s = lax.rem(me + j, n)
+        return pltpu.make_async_remote_copy(
+            src_ref=qsum.at[s],
+            dst_ref=qpart.at[me],
+            send_sem=qpart_send.at[j],
+            recv_sem=qpart_recv.at[me],
+            device_id={"blk": s},
+            device_id_type=MESH,
+        )
+
+    def out_copy(z0, y0):
         first = pl.multiple_of(index(z0, y0, 0) * rows, 2 * rows)
-        slot = lax.rem(gi, 2)
+        slot = z0 * lines + y0
         return pltpu.make_async_copy(
             stage.at[slot], scores_ref.at[:, pl.ds(first, 2 * rows)], out_sem.at[slot]
         )
 
-    def score(gi, z0, y0):
-        @pl.loop(0, CHUNKS)
-        def _(h):
-            arrived(z0, y0, 1 - c, h)
-
-        @pl.when(gi >= 2)
-        def _():
-            out_copy(gi, z0, y0).wait()
-
-        first = pl.multiple_of(index(z0, y0, 0) * rows, 2 * rows)
-        stage[lax.rem(gi, 2)] = dot(qb[...], held[pl.ds(first, 2 * rows), :], NT)
-        out_copy(gi, z0, y0).start()
+    def score(far, y0):
+        @pl.loop(0, 2)
+        def _(i):
+            z0 = z + (1 - 2 * i) * far
+
+            @pl.when(jnp.logical_and(inside(z0), jnp.logical_or(i == 0, far > 0)))
+            def _():
+                @pl.loop(0, CHUNKS)
+                def _(h):
+                    arrived(z0, y0, 1 - c, h)
+
+                first = pl.multiple_of(index(z0, y0, 0) * rows, 2 * rows)
+                stage[z0 * lines + y0] = dot(qb[...], held[pl.ds(first, 2 * rows), :], NT)
+                out_copy(z0, y0).start()
 
     own_copy.wait()
 
@@ -248,25 +268,27 @@
     def _(k):
         step = lax.div(k, CHUNKS)
         h = lax.rem(k, CHUNKS)
-        z_line = order(step)
-
-        @pl.when(step < depth - 1)
-        def _():
-            arrived(z_line, y, c, h)
-            send_z(z_line, y, h)
-            send_y(z_line, y, h)
-            send_twin(z_line, y, h)
+        for side in (1, -1):
+            z_line = z + side * (step + 1)
+
+            @pl.when(inside(z_line))
+            def _():
+                arrived(z_line, y, c, h)
+                send_z(z_line, y, h)
+                send_y(z_line, y, h)
+                send_twin(z_line, y, h)
 
         if lines == 2:
-            z_cross = jnp.where(step == 0, z, order(step - 1))
-            by_z = jnp.logical_and(
-                jnp.logical_or(z_cross == z + 1, z_cross == z - 1), h < crossed
-            )
-
-            @pl.when(jnp.logical_not(by_z))
-            def _():
-                arrived(z_cross, 1 - y, c, h)
-                send_twin(z_cross, 1 - y, h)
+            for side in (1, -1):
+                z_cross = z + side * step
+                wanted = jnp.logical_or(step > 1, jnp.logical_or(step == 0, h >= crossed))
+                if side == -1:
+                    wanted = jnp.logical_and(wanted, step > 0)
+
+                @pl.when(jnp.logical_and(wanted, inside(z_cross)))
+                def _():
+                    arrived(z_cross, 1 - y, c, h)
+                    send_twin(z_cross, 1 - y, h)
 
             @pl.when(k == slots - CHUNKS)
             def _():
@@ -288,14 +310,36 @@
 
         @pl.when(k == spin)
         def _():
-            share(qsum, qsum_send, qsum_recv)
+            @pl.loop(1, n)
+            def _(j):
+                part_to(j).start()
+
+        @pl.when(k == spin + 1)
+        def _():
+            @pl.loop(1, n)
+            def _(j):
+                s = lax.rem(me + j, n)
+                pltpu.make_async_remote_copy(
+                    src_ref=qsum.at[s],
+                    dst_ref=qpart.at[s],
+                    send_sem=qpart_send.at[j],
+                    recv_sem=qpart_recv.at[s],
+                    device_id={"blk": s},
+                    device_id_type=MESH,
+                ).wait_recv()
+                part_to(j).wait_send()
+
+            qpart[me] = qsum[me]
+            added = qpart[0]
+            for s in range(1, n):
+                added = added + qpart[s]
+            qtotal[me] = added
+            share(qtotal, qsum_send, qsum_recv)
 
         @pl.when(k == spin + 2)
         def _():
-            collect(qsum, qsum_send, qsum_recv)
-            total = qsum[0]
-            for s in range(1, n):
-                total = total + qsum[s]
+            collect(qtotal, qsum_send, qsum_recv)
+            total = jnp.concatenate([qtotal[s] for s in range(n)], axis=1)
             high = total.astype(BF16)
             rest = total - high.astype(F32)
             middle = rest.astype(BF16)
@@ -310,26 +354,21 @@
             share(csum, csum_send, csum_recv)
 
         early = k - spin
-        use_own = early == 0
-        use_first = jnp.logical_and(early >= 1, early <= 2)
-        use_line = jnp.logical_and(
-            early >= 3, jnp.logical_and(h == CHUNKS - 1, step < depth - 1)
-        )
-        chosen = jnp.where(use_first, early - 1, step)
-        z_score = jnp.where(use_own, z, order(chosen))
-        gi = jnp.where(use_own, 0, chosen + 1)
-        use = jnp.logical_or(use_own, jnp.logical_or(use_first, use_line))
+        by_arrival = jnp.logical_and(
+            early > 2, jnp.logical_and(h == CHUNKS - 1, step + 1 < depth)
+        )
+        far = jnp.where(early > 2, step + 1, early)
+        use = jnp.logical_or(jnp.logical_and(early >= 0, early <= 2), by_arrival)
         y_score = y
         if lines == 2:
-            use_cross = k == slots - CHUNKS
-            z_score = jnp.where(use_cross, z, z_score)
-            y_score = jnp.where(use_cross, 1 - y, y)
-            gi = jnp.where(use_cross, depth, gi)
-            use = jnp.logical_or(use, use_cross)
+            other = jnp.logical_or(k == spin + CHUNKS, k == spin + CHUNKS + 1)
+            far = jnp.where(k == spin + CHUNKS, 0, jnp.where(k == spin + CHUNKS + 1, 2, far))
+            y_score = jnp.where(other, 1 - y, y)
+            use = jnp.logical_or(use, other)
 
         @pl.when(use)
         def _():
-            score(gi, z_score, y_score)
+            score(far, y_score)
 
     if lines == 2:
         for side in (1, -1):
@@ -341,9 +380,9 @@
                     arrived(z + side, 1 - y, c, h)
                     send_twin(z + side, 1 - y, h)
 
-        @pl.loop(0, depth - 1)
+        @pl.loop(0, 2)
         def _(j):
-            score(depth + 1 + j, order(depth - 2 - j), 1 - y)
+            score(3 - 2 * j, 1 - y)
 
     collect(csum, csum_send, csum_recv)
     ids = (
@@ -354,14 +393,11 @@
         picked = picked + jnp.where(smalls[s, per - 1 : per, :] == ids, csum[s], 0.0)
     totals_ref[...] = jnp.sum(picked.T, axis=0, keepdims=True)
 
-    done = depth * lines
-    out_copy(done, z, y).wait()
-    out_copy(done + 1, z, y).wait()
-
     @pl.loop(0, depth * lines)
     def _(s):
         z0 = lax.div(s, lines)
         y0 = lax.rem(s, lines)
+        out_copy(z0, y0).wait()
 
         @pl.loop(0, CHUNKS)
         def _(h):
@@ -387,13 +423,6 @@
 def per_device(n, lines, query_sketch, train_sketch, train_ids, basis_in, basis_out, eig_in, eig_out):
     width = FOUT * FIN
     queries, rows = query_sketch.shape[0], train_sketch.shape[0]
-    scale = (
-        1.0 / (eig_out[:, None] * eig_in[None, :] + 0.01) / jnp.sqrt(jnp.float32(width))
-    ).reshape(1, width)
-    both = jnp.concatenate([basis_in, basis_out], axis=1).astype(F32)
-    small = jnp.concatenate(
-        [both, jnp.zeros((7 - both.shape[0], 128), F32), train_ids.astype(F32)[None, :]], axis=0
-    )
     sources = n // 2
     dma = pltpu.SemaphoreType.DMA
     vmem = pl.BlockSpec(memory_space=pltpu.VMEM)
@@ -404,7 +433,7 @@
             jax.ShapeDtypeStruct((queries, rows * n), F32),
             jax.ShapeDtypeStruct((1, rows), F32),
         ),
-        in_specs=[hbm, hbm, vmem, vmem],
+        in_specs=[hbm, hbm, vmem, vmem, vmem, vmem, pl.BlockSpec(memory_space=pltpu.SMEM)],
         out_specs=(hbm, vmem),
         scratch_shapes=[
             pltpu.VMEM((n * rows, width), BF16),
@@ -412,11 +441,14 @@
             pltpu.VMEM((queries, width), BF16),
             pltpu.VMEM((width, LANES), BF16),
             pltpu.VMEM((2, FOUT, width), F32),
+            pltpu.VMEM((1, width), F32),
             pltpu.VMEM((2, LANES, LANES), BF16),
-            pltpu.VMEM((2, queries, 2 * rows), F32),
+            pltpu.VMEM((sources, queries, 2 * rows), F32),
             pltpu.VMEM((FIN, 128), F32),
             pltpu.VMEM((n, 8, 128), F32),
-            pltpu.VMEM((n, 1, width), F32),
+            pltpu.VMEM((n, 1, width // n), F32),
+            pltpu.VMEM((n, 1, width // n), F32),
+            pltpu.VMEM((n, 1, width // n), F32),
             pltpu.VMEM((n, 1, rows), F32),
             dma((n * CHUNKS,)),
             dma((4, sources * CHUNKS)),
@@ -426,8 +458,10 @@
             dma((n,)),
             dma((n,)),
             dma((n,)),
+            dma((n,)),
+            dma((n,)),
             dma((2,)),
-            dma((2,)),
+            dma((sources,)),
         ],
         compiler_params=pltpu.CompilerParams(
             collective_id=0, has_side_effects=True, vmem_limit_bytes=58 * 1024 * 1024
@@ -437,7 +471,10 @@
             bytes_accessed=2 * queries * width + 4 * queries * rows * n,
             transcendentals=0,
         ),
-    )(query_sketch, train_sketch, small, scale)
+    )(
+        query_sketch, train_sketch, basis_in, basis_out,
+        train_ids.reshape(1, rows), eig_in.reshape(1, FIN), eig_out.reshape(1, FOUT),
+    )
     return scores, totals.reshape(rows)
 
 

time: 121 us -> 113 us (0.934)
  the two profiles are of different devices: /device:TPU:9 before, /device:TPU:17 now
where the time goes in v2:
time: 113 us
  Pallas kernels  107 us (95%)
  local copies, waits for them, and re-layouts  5.21 us (5%)
    pallas_call x1, Pallas kernels, per_device(): pl.pallas_call(functools.partial(kernel, n, lines), out_shape=(jax.ShapeD...  107 us
    unnamed x4, local copies, waits for them, and re-layouts  5.21 us

profile of v2, /device:TPU:17, one launch (start us, length us, event | category | flops | bytes accessed | tf_op | source)
XLA Modules:
  0.0 112.9 jit_solution(12028616123073059727)
XLA Ops:
  0.6 107.0 %shard_map.86 = (f32[512,2048]{1,0:T(8,128)}, f32[1,128]{1,0:T(1,128)}) custom-call(bf16[512,4096]{1,0:T(8,128)(2,1)} %q_ref.1, bf16[128,4096]{1,0:T(8,128)(2,1)} %t_ref.1, bf16[4,64]{1,0:T(4,128)(2,1)} %in_ref.1, bf16[4,64]{1,0:T(4,128)(2,1)} %out_ref.1, s32[1,128]{1,0:T(1,128)} %bitcast.4, f32[1,64]{1,0:T(1,128)} %bitcast.5, f32[1,64]{1,0:T(1,128)} %bitcast.6), custom_call_target="tpu_custom_call" | custom-call | flops 42949672960 | bytes 8388608 | tf_op jit(solution)/shard_map/pallas_call | solution.py:430
  107.7 0.0 copy-start
  107.7 4.7 %copy.11 = f32[512,2048]{1,0:T(8,128)} copy(f32[512,2048]{1,0:T(8,128)} %get-tuple-element.8) | data formatting | bytes 8388608
  112.4 0.0 copy-done
  112.4 0.5 copy.12
Async XLA Ops:
  107.7 4.7 %copy-start = (f32[1,128]{1,0:T(1,128)S(1)}, f32[1,128]{1,0:T(1,128)}, u32[]{:S(2)}) copy-start(f32[1,128]{1,0:T(1,128)} %get-tuple-element.5) | copy-start | bytes 1540

commit v3 on v2

--- a/solution.py
+++ b/solution.py
@@ -314,7 +314,7 @@
             def _(j):
                 part_to(j).start()
 
-        @pl.when(k == spin + 1)
+        @pl.when(k == spin + CHUNKS)
         def _():
             @pl.loop(1, n)
             def _(j):
@@ -336,7 +336,7 @@
             qtotal[me] = added
             share(qtotal, qsum_send, qsum_recv)
 
-        @pl.when(k == spin + 2)
+        @pl.when(k == spin + 2 * CHUNKS - 1)
         def _():
             collect(qtotal, qsum_send, qsum_recv)
             total = jnp.concatenate([qtotal[s] for s in range(n)], axis=1)

time: 113 us -> 110 us (0.973)
  the two profiles are of different devices: /device:TPU:17 before, /device:TPU:0 now
where the time goes in v3:
time: 110 us
  Pallas kernels  104 us (95%)
  local copies, waits for them, and re-layouts  5.21 us (5%)
    pallas_call x1, Pallas kernels, per_device(): pl.pallas_call(functools.partial(kernel, n, lines), out_shape=(jax.ShapeD...  104 us
    unnamed x4, local copies, waits for them, and re-layouts  5.21 us

profile of v3, /device:TPU:0, one launch (start us, length us, event | category | flops | bytes accessed | tf_op | source)
XLA Modules:
  0.0 110.1 jit_solution(4905640544003689752)
XLA Ops:
  0.6 104.3 %shard_map.86 = (f32[512,2048]{1,0:T(8,128)}, f32[1,128]{1,0:T(1,128)}) custom-call(bf16[512,4096]{1,0:T(8,128)(2,1)} %q_ref.1, bf16[128,4096]{1,0:T(8,128)(2,1)} %t_ref.1, bf16[4,64]{1,0:T(4,128)(2,1)} %in_ref.1, bf16[4,64]{1,0:T(4,128)(2,1)} %out_ref.1, s32[1,128]{1,0:T(1,128)} %bitcast.4, f32[1,64]{1,0:T(1,128)} %bitcast.5, f32[1,64]{1,0:T(1,128)} %bitcast.6), custom_call_target="tpu_custom_call" | custom-call | flops 42949672960 | bytes 8388608 | tf_op jit(solution)/shard_map/pallas_call | solution.py:430
  104.9 0.0 copy-start
  104.9 4.7 %copy.11 = f32[512,2048]{1,0:T(8,128)} copy(f32[512,2048]{1,0:T(8,128)} %get-tuple-element.8) | data formatting | bytes 8388608
  109.6 0.0 copy-done
  109.6 0.5 copy.12
Async XLA Ops:
  104.9 4.7 %copy-start = (f32[1,128]{1,0:T(1,128)S(1)}, f32[1,128]{1,0:T(1,128)}, u32[]{:S(2)}) copy-start(f32[1,128]{1,0:T(1,128)} %get-tuple-element.5) | copy-start | bytes 1540
